TPU v7x, 128 devices: a whole 4x4x4 slice. The times are simulated.
128 devices in a mesh: gx: 8 (over z, core), yz: 16 (over x, y).
Axes of the slice: x: 4, y: 4, z: 4, core: 2. Of those that a mesh axis runs over, the one named last changes fastest.
Arguments:
- features: bfloat16 [768, 64, 4096], P(('gx', 'yz')), may hold values from -6 to 6
- brick_state: int32 [768], P(('gx', 'yz')), may hold values from -1 to 2, as said below
- neighbor: int32 [768, 6], P(('gx', 'yz')), may hold values from -1 to 11, as said below
- w_first: bfloat16 [27, 64, 64], replicated, may hold values from -0.15625 to 0.15625
- b_first: float32 [64], replicated, may hold values from -3 to 3
- w_second: bfloat16 [27, 64, 64], replicated, may hold values from -0.15625 to 0.15625
- b_second: float32 [64], replicated, may hold values from -3 to 3
Outputs:
- blocks: bfloat16 [768, 64, 4096], P(('gx', 'yz'))
Inputs may be any that keep to these rules, and one draw needn't show every extreme that they name: `brick_state`: per slot: -1 empty; 0 occupied and computed by its own region; 1 occupied and lent to the region at yz - 1 of the same slab; 2 lent to the region at yz + 1. A region lends at most 1 bricks to each side, and the bricks it computes (its code-0 bricks and those lent to it) number at most 4; both bounds are reached in every draw, and some region has all 6 slots occupied. `neighbor`: per slot and face (x-, x+, y-, y+, z-, z+): -1 if the slot is empty or no occupied brick touches that face; k < 6 names slot k of the same region; k >= 6 names slot k - 6 of the adjacent region across that face (gx - 1, gx + 1, yz - 1, yz + 1 for the four side faces; z faces never leave the region). Entries point only at occupied slots and adjacency is symmetric.
All inputs are finite; a program needn't handle non-finite values.
Results may differ from a plain program's by a relative error of at most 0.0049.
Values may be sent and summed in bfloat16 or wider, within the bound.
A program may use at most 192 MiB of HBM per device.

v0:
```python
import jax
import jax.numpy as jnp
from jax import lax
from jax.sharding import PartitionSpec as P

EDGE = 16
LEND = 1
HOLD = 4


def with_halo(x, sides, width):
    for axis, dim in sides:
        size, length = (lax.axis_size(axis), x.shape[dim])
        up = [(i, (i + 1) % size) for i in range(size - 1)]
        down = [(j, i) for i, j in up]
        last = lax.slice_in_dim(x, length - width, length, axis=dim)
        leading = lax.slice_in_dim(x, 0, width, axis=dim)
        before = lax.ppermute(last, axis, up)
        after = lax.ppermute(leading, axis, down)
        x = jnp.concatenate([before, x, after], axis=dim)
    return x


def ranked(wanted, needed):
    position = jnp.cumsum(wanted.astype(jnp.int32)) - 1
    matches = wanted[None, :] & (position[None, :] == jnp.arange(needed, dtype=jnp.int32)[:, None])
    chosen = jnp.sum(
        jnp.where(matches, jnp.arange(wanted.shape[0], dtype=jnp.int32)[None, :], 0), axis=1
    )
    return (chosen, jnp.any(matches, axis=1))


def kernel_of(weights):
    channels = weights.shape[1]
    return weights.reshape(3, 3, 3, channels, channels).transpose(3, 4, 0, 1, 2)


def planes_of(values):
    bricks, channels = (values.shape[0], values.shape[1])
    volume = values.reshape(bricks, channels, EDGE, EDGE, EDGE)
    face_sheets = [
        volume[:, :, 0],
        volume[:, :, -1],
        volume[:, :, :, 0],
        volume[:, :, :, -1],
        volume[:, :, :, :, 0],
        volume[:, :, :, :, -1],
    ]
    return jnp.stack(
        [face_sheet.reshape(bricks, channels, EDGE * EDGE) for face_sheet in face_sheets], axis=1
    )


def facing(planes, neighbor):
    across_x = with_halo(planes[:, 0:2], (("gx", 1),), 1)
    across_y = with_halo(planes[:, 2:4], (("yz", 1),), 1)
    tables = [
        jnp.concatenate([planes[:, 1], across_x[:, 0]], axis=0),
        jnp.concatenate([planes[:, 0], across_x[:, 3]], axis=0),
        jnp.concatenate([planes[:, 3], across_y[:, 0]], axis=0),
        jnp.concatenate([planes[:, 2], across_y[:, 3]], axis=0),
        jnp.concatenate([planes[:, 5], planes[:, 5]], axis=0),
        jnp.concatenate([planes[:, 4], planes[:, 4]], axis=0),
    ]
    gathered = []
    for face_index in range(6):
        wanted = neighbor[:, face_index]
        source = tables[face_index]
        picked = jnp.take(source, jnp.clip(wanted, 0, source.shape[0] - 1), axis=0)
        gathered.append(jnp.where((wanted >= 0)[:, None, None], picked, jnp.zeros_like(picked)))
    return jnp.stack(gathered, axis=1)


def padded_of(values, halos):
    bricks, channels = (values.shape[0], values.shape[1])
    padded_side = EDGE + 2
    volume = values.reshape(bricks, channels, EDGE, EDGE, EDGE)
    sheets = halos.reshape(bricks, 6, channels, EDGE, EDGE)
    core = jnp.concatenate([sheets[:, 4][..., None], volume, sheets[:, 5][..., None]], axis=4)
    side_pad = ((0, 0), (0, 0), (0, 0), (1, 1))
    lower_y = jnp.pad(sheets[:, 2], side_pad)[:, :, :, None, :]
    upper_y = jnp.pad(sheets[:, 3], side_pad)[:, :, :, None, :]
    core = jnp.concatenate([lower_y, core, upper_y], axis=3)
    face_pad = ((0, 0), (0, 0), (1, 1), (1, 1))
    lower_x = jnp.pad(sheets[:, 0], face_pad)[:, :, None]
    upper_x = jnp.pad(sheets[:, 1], face_pad)[:, :, None]
    full = jnp.concatenate([lower_x, core, upper_x], axis=2)
    return full.reshape(bricks, channels, padded_side**3)


def convolve(padded, kernel, bias_row):
    bricks, channels = (padded.shape[0], padded.shape[1])
    padded_side = EDGE + 2
    cubes = padded.reshape(bricks, channels, padded_side, padded_side, padded_side)
    result = lax.conv_general_dilated(
        cubes,
        kernel,
        (1, 1, 1),
        "VALID",
        dimension_numbers=("NCDHW", "OIDHW", "NCDHW"),
        preferred_element_type=jnp.float32,
    )
    return result.reshape(bricks, channels, EDGE**3) + bias_row[None, :, None]


def lending_plan(brick_state):
    beside_states = with_halo(brick_state[None, :], (("yz", 0),), 1)
    to_left, unused_left = ranked(brick_state == 1, LEND)
    to_right, unused_right = ranked(brick_state == 2, LEND)
    slots_left, from_left = ranked(beside_states[0] == 2, LEND)
    slots_right, from_right = ranked(beside_states[2] == 1, LEND)
    candidate = jnp.concatenate([brick_state == 0, from_left, from_right])
    hold_source, unused_hold = ranked(candidate, HOLD)
    hold_place = jnp.clip(jnp.cumsum(candidate.astype(jnp.int32)) - 1, 0, HOLD - 1)
    first_rank = jnp.cumsum((brick_state == 1).astype(jnp.int32)) - 1
    second_rank = jnp.cumsum((brick_state == 2).astype(jnp.int32)) - 1
    lent_place = jnp.clip(
        jnp.where(brick_state == 1, first_rank, LEND + second_rank), 0, 2 * LEND - 1
    )
    return (jnp.concatenate([to_left, to_right]), hold_source, hold_place, lent_place)


def lend(padded_all, lend_slots):
    outgoing = jnp.take(padded_all, lend_slots, axis=0)
    outgoing = outgoing.reshape((2, LEND) + outgoing.shape[1:])
    arrived = with_halo(outgoing, (("yz", 0),), 1)
    return jnp.concatenate([arrived[0], arrived[3]], axis=0)


def send_home(going):
    going = going.reshape((2, LEND) + going.shape[1:])
    returned = with_halo(going, (("yz", 0),), 1)
    return jnp.concatenate([returned[0], returned[3]], axis=0)


def run_held(candidates, hold_source, hold_place, kernel, bias_row, activate):
    held_bricks = jnp.take(candidates, hold_source, axis=0)
    result = convolve(held_bricks, kernel, bias_row)
    if activate:
        result = jax.nn.relu(result)
    return jnp.take(result.astype(jnp.bfloat16), hold_place, axis=0)


def settle(own_rows, lent_rows, brick_state, lent_place):
    arrived_rows = jnp.take(lent_rows, lent_place, axis=0)
    kept_here = (brick_state == 0)[:, None, None]
    lent_away = (brick_state > 0)[:, None, None]
    return jnp.where(
        kept_here, own_rows, jnp.where(lent_away, arrived_rows, jnp.zeros_like(arrived_rows))
    )


def per_device(features, brick_state, neighbor, w_first, b_first, w_second, b_second):
    owned = features.shape[0]
    occupied = (brick_state >= 0)[:, None, None]
    first_kernel = kernel_of(w_first)
    second_kernel = kernel_of(w_second)
    padded_first = padded_of(features, facing(planes_of(features), neighbor))
    lend_slots, hold_source, hold_place, lent_place = lending_plan(brick_state)
    arrived = lend(padded_first, lend_slots)
    back_first = run_held(
        jnp.concatenate([padded_first, arrived], axis=0),
        hold_source,
        hold_place,
        first_kernel,
        b_first,
        True,
    )
    hidden = settle(back_first[:owned], send_home(back_first[owned:]), brick_state, lent_place)
    padded_second = padded_of(hidden, facing(planes_of(hidden), neighbor))
    arrived_second = lend(padded_second, lend_slots)
    back_second = run_held(
        jnp.concatenate([padded_second, arrived_second], axis=0),
        hold_source,
        hold_place,
        second_kernel,
        b_second,
        False,
    )
    branch = settle(back_second[:owned], send_home(back_second[owned:]), brick_state, lent_place)
    summed = features.astype(jnp.float32) + branch.astype(jnp.float32)
    return jnp.where(occupied, jax.nn.relu(summed), 0.0).astype(jnp.bfloat16)


def solution(mesh):
    in_specs = (
        P(("gx", "yz"), None, None),
        P(("gx", "yz")),
        P(("gx", "yz"), None),
        P(),
        P(),
        P(),
        P(),
    )
    out_specs = P(("gx", "yz"), None, None)
    return jax.shard_map(
        per_device, mesh=mesh, in_specs=in_specs, out_specs=out_specs, check_vma=False
    )
```

profile of v0, /device:TPU:24, one launch (start us, length us, event | category | flops | bytes accessed | tf_op | source)
XLA Modules:
  0.0 636.0 jit_solution(11200909150304730811)
XLA Ops:
  6.0 6.6 %copy.64 = bf16[6,64,4096]{1,2,0:T(8,128)(2,1)} copy(bf16[6,64,4096]{2,1,0:T(8,128)(2,1)} %param.17) | data formatting | bytes 6291456 | tf_op args[0]
  66.0 11.0 %pad_maximum_fusion = bf16[6,64,18,18,18]{1,4,3,2,0:T(8,128)(2,1)} fusion(bf16[6,64,1,18,18]{1,4,3,2,0:T(8,128)(2,1)S(1)} %pad_bitcast_fusion.2, bf16[6,64,16,1,18]{1,4,3,2,0:T(8,128)(2,1)} %pad_bitcast_fusion.6, bf16[6,64,16,16,1]{1,4,3,2,0:T(2,128)(2,1)S(1)} %copy.67, bf16[6,64,16,16,16]{1,4,3,2,0:T(8,128)(2,1)} %bitcast.168, ...), kind=kLoop, calls=%fused_computation.31 | loop fusion | flops 31352832 | bytes 8957952 | tf_op jit(solution)/shard_map/concatenate | solution.py:87
  77.0 16.1 %reshape.341 = bf16[6,64,5832]{1,2,0:T(8,128)(2,1)} reshape(bf16[6,64,18,18,18]{1,4,3,2,0:T(8,128)(2,1)} %pad_maximum_fusion) | data formatting | bytes 8957952 | tf_op jit(solution)/shard_map/reshape | solution.py:88
  100.4 6.0 collective-permute-start.4
  111.0 12.0 %collective-permute-done.4 = bf16[1,1,64,5832]{3,2,1,0:T(8,128)(2,1)S(1)} collective-permute-done((bf16[1,1,64,5832]{3,2,1,0:T(8,128)(2,1)}, bf16[1,1,64,5832]{3,2,1,0:T(8,128)(2,1)S(1)}, u32[]{:S(2)}, u32[]{:S(2)}) %collective-permute-start.4) | collective-permute-done | bytes 746528 | tf_op jit(solution)/shard_map/ppermute | solution.py:18
  124.4 6.6 %collective-permute-done.5 = bf16[1,1,64,5832]{3,2,1,0:T(8,128)(2,1)} collective-permute-done((bf16[1,1,64,5832]{3,2,1,0:T(8,128)(2,1)S(1)}, bf16[1,1,64,5832]{3,2,1,0:T(8,128)(2,1)}, u32[]{:S(2)}, u32[]{:S(2)}) %collective-permute-start.5) | collective-permute-done | bytes 746528 | tf_op jit(solution)/shard_map/ppermute | solution.py:19
  133.3 10.0 %pad_maximum_fusion.1 = bf16[8,64,5832]{1,2,0:T(8,128)(2,1)} fusion(bf16[1,64,5832]{1,2,0:T(8,128)(2,1)S(1)} %bitcast.181, bf16[1,64,5832]{1,2,0:T(8,128)(2,1)S(1)} %bitcast.179, bf16[6,64,5832]{1,2,0:T(8,128)(2,1)} %reshape.341), kind=kLoop, calls=%fused_computation.32 | loop fusion | flops 5971968 | bytes 11943936 | tf_op jit(solution)/shard_map/concatenate | solution.py:162
  143.3 8.2 %gather_fusion.7 = bf16[4,64,5832]{1,2,0:T(8,128)(2,1)} fusion(bf16[8,64,5832]{1,2,0:T(8,128)(2,1)} %pad_maximum_fusion.1, s32[1024]{0:T(1024)S(1)} %pad_clamp_fusion.2), kind=kCustom, calls=%fused_computation.2.clone | custom fusion | bytes 5971984 | tf_op jit(solution)/shard_map/jit(_take)/gather | solution.py:137
  154.8 22.6 %copy.75 = bf16[4,64,5832]{1,0,2:T(4,128)(2,1)} copy(bf16[4,64,5832]{1,2,0:T(8,128)(2,1)S(1)} %broadcast_select_fusion.2) | data formatting | bytes 5971968 | tf_op jit(solution)/shard_map/jit(_take)/select_n | solution.py:137
  177.4 10.0 %pad.34 = bf16[64,18,18,4,24]{0,3,4,2,1:T(4,128)(2,1)} pad(bf16[64,18,18,4,18]{0,3,4,2,1:T(4,128)(2,1)} %bitcast.178, bf16[]{:T(256)} %constant.68.clone.1), padding=0_0x0_0x0_0x0_0x0_6 | pad | bytes 6967298 | tf_op jit(solution)/shard_map/reshape | solution.py:94
  192.1 8.2 %fusion.2 = bf16[64,18,18,4,8,5]{0,3,5,4,2,1:T(4,128)(2,1)} fusion(bf16[64,18,18,4,7,2]{0,3,5,4,2,1:T(4,128)(2,1)S(1)} %slice.240, bf16[64,18,18,4,8,3]{0,3,5,4,2,1:T(4,128)(2,1)S(1)} %bitcast.164), kind=kLoop, calls=%fused_computation.23 | loop fusion | flops 19906560 | bytes 12939264 | tf_op jit(solution)/shard_map/conv_general_dilated | solution.py:95
  200.3 51.5 %broadcast_select_fusion.1 = f32[16,16,32,3,64]{4,2,3,1,0:T(8,128)} fusion(pred[32,3]{0,1:T(4,128)(4,1)S(1)} %copy-done.14, bf16[3,3,3,64,64]{4,3,2,1,0:T(8,128)(2,1)S(1)} %bitcast.160, bf16[64,18,18,4,8,5]{0,3,5,4,2,1:T(4,128)(2,1)} %fusion.2), kind=kOutput, calls=%fused_computation.38 | convolution fusion | flops 5437390848 | bytes 13148256 | tf_op jit(solution)/shard_map/conv_general_dilated | solution.py:95
  251.8 18.9 %copy.77 = f32[16,16,32,3,64]{4,1,3,2,0:T(8,128)} copy(f32[16,16,32,3,64]{4,2,3,1,0:T(8,128)} %broadcast_select_fusion.1) | data formatting | bytes 12582912 | tf_op jit(solution)/shard_map/conv_general_dilated | solution.py:95
  274.6 7.3 %copy.78 = f32[4,64,16,16,16]{1,4,3,2,0:T(8,128)} copy(f32[4,64,16,16,16]{1,3,4,0,2:T(8,128)S(1)} %slice_bitcast_fusion.1) | data formatting | bytes 8388608 | tf_op jit(solution)/shard_map/conv_general_dilated | solution.py:95
  281.9 6.8 %copy.79 = f32[4,64,4096]{2,1,0:T(8,128)} copy(f32[4,64,4096]{1,2,0:T(8,128)} %bitcast.175) | data formatting | bytes 8388608 | tf_op jit(solution)/shard_map/reshape | solution.py:103
  304.6 10.4 %collective-permute-done.8 = bf16[1,1,64,4096]{3,2,1,0:T(8,128)(2,1)S(1)} collective-permute-done((bf16[1,1,64,4096]{3,2,1,0:T(8,128)(2,1)S(1)}, bf16[1,1,64,4096]{3,2,1,0:T(8,128)(2,1)S(1)}, u32[]{:S(2)}, u32[]{:S(2)}) %collective-permute-start.8) | collective-permute-done | bytes 524320 | tf_op jit(solution)/shard_map/ppermute | solution.py:18
  326.6 6.6 %copy.80 = bf16[6,64,4096]{1,2,0:T(8,128)(2,1)} copy(bf16[6,64,4096]{2,1,0:T(8,128)(2,1)} %slice_select_fusion.1) | data formatting | bytes 6291456 | tf_op jit(solution)/shard_map/jit(_where)/select_n | solution.py:148
  378.0 11.0 %pad_maximum_fusion.2 = bf16[6,64,18,18,18]{1,4,3,2,0:T(8,128)(2,1)} fusion(bf16[6,64,1,18,18]{1,4,3,2,0:T(8,128)(2,1)S(1)} %pad_bitcast_fusion, bf16[6,64,16,1,18]{1,4,3,2,0:T(8,128)(2,1)} %pad_bitcast_fusion.4, bf16[6,64,16,16,1]{1,4,3,2,0:T(2,128)(2,1)S(1)} %copy.83, bf16[6,64,16,16,16]{1,4,3,2,0:T(8,128)(2,1)} %bitcast.172, ...), kind=kLoop, calls=%fused_computation.33 | loop fusion | flops 31352832 | bytes 8957952 | tf_op jit(solution)/shard_map/concatenate | solution.py:87
  389.0 16.1 %reshape.349 = bf16[6,64,5832]{1,2,0:T(8,128)(2,1)} reshape(bf16[6,64,18,18,18]{1,4,3,2,0:T(8,128)(2,1)} %pad_maximum_fusion.2) | data formatting | bytes 8957952 | tf_op jit(solution)/shard_map/reshape | solution.py:88
  420.2 13.3 %collective-permute-done.14 = bf16[1,1,64,5832]{3,2,1,0:T(8,128)(2,1)S(1)} collective-permute-done((bf16[1,1,64,5832]{3,2,1,0:T(8,128)(2,1)}, bf16[1,1,64,5832]{3,2,1,0:T(8,128)(2,1)S(1)}, u32[]{:S(2)}, u32[]{:S(2)}) %collective-permute-start.14) | collective-permute-done | bytes 746528 | tf_op jit(solution)/shard_map/ppermute | solution.py:18
  435.0 6.0 collective-permute-done.15
  443.3 10.0 %pad_maximum_fusion.3 = bf16[8,64,5832]{1,2,0:T(8,128)(2,1)} fusion(bf16[1,64,5832]{1,2,0:T(8,128)(2,1)S(1)} %bitcast.182, bf16[1,64,5832]{1,2,0:T(8,128)(2,1)S(1)} %bitcast.180, bf16[6,64,5832]{1,2,0:T(8,128)(2,1)} %reshape.349), kind=kLoop, calls=%fused_computation.34 | loop fusion | flops 5971968 | bytes 11943936 | tf_op jit(solution)/shard_map/concatenate | solution.py:173
  453.3 8.2 %gather_fusion.17 = bf16[4,64,5832]{1,2,0:T(8,128)(2,1)} fusion(bf16[8,64,5832]{1,2,0:T(8,128)(2,1)} %pad_maximum_fusion.3, s32[1024]{0:T(1024)S(1)} %pad_clamp_fusion.2), kind=kCustom, calls=%fused_computation.17.clone | custom fusion | bytes 5971984 | tf_op jit(solution)/shard_map/jit(_take)/gather | solution.py:137
  464.8 22.6 %copy.91 = bf16[4,64,5832]{1,0,2:T(4,128)(2,1)} copy(bf16[4,64,5832]{1,2,0:T(8,128)(2,1)S(1)} %broadcast_select_fusion.3) | data formatting | bytes 5971968 | tf_op jit(solution)/shard_map/jit(_take)/select_n | solution.py:137
  487.4 10.0 %pad.36 = bf16[64,18,18,4,24]{0,3,4,2,1:T(4,128)(2,1)} pad(bf16[64,18,18,4,18]{0,3,4,2,1:T(4,128)(2,1)} %bitcast.177, bf16[]{:T(256)} %constant.68.clone.1), padding=0_0x0_0x0_0x0_0x0_6 | pad | bytes 6967298 | tf_op jit(solution)/shard_map/reshape | solution.py:94
  502.1 8.2 %fusion.3 = bf16[64,18,18,4,8,5]{0,3,5,4,2,1:T(4,128)(2,1)} fusion(bf16[64,18,18,4,7,2]{0,3,5,4,2,1:T(4,128)(2,1)S(1)} %slice.253, bf16[64,18,18,4,8,3]{0,3,5,4,2,1:T(4,128)(2,1)S(1)} %bitcast.162), kind=kLoop, calls=%fused_computation.24 | loop fusion | flops 19906560 | bytes 12939264 | tf_op jit(solution)/shard_map/conv_general_dilated | solution.py:95
  510.3 51.3 %broadcast_select_fusion = f32[16,16,32,3,64]{4,2,3,1,0:T(8,128)} fusion(pred[32,3]{0,1:T(4,128)(4,1)S(1)} %copy-done.15, bf16[3,3,3,64,64]{4,3,2,1,0:T(8,128)(2,1)S(1)} %bitcast.215, bf16[64,18,18,4,8,5]{0,3,5,4,2,1:T(4,128)(2,1)} %fusion.3), kind=kOutput, calls=%fused_computation.37 | convolution fusion | flops 5437390848 | bytes 13148256 | tf_op jit(solution)/shard_map/conv_general_dilated | solution.py:95
  561.6 18.9 %copy.93 = f32[16,16,32,3,64]{4,1,3,2,0:T(8,128)} copy(f32[16,16,32,3,64]{4,2,3,1,0:T(8,128)} %broadcast_select_fusion) | data formatting | bytes 12582912 | tf_op jit(solution)/shard_map/conv_general_dilated | solution.py:95
  584.4 7.4 %copy.94 = f32[4,64,16,16,16]{1,4,3,2,0:T(8,128)} copy(f32[4,64,16,16,16]{1,3,4,0,2:T(8,128)S(1)} %slice_bitcast_fusion) | data formatting | bytes 8388608 | tf_op jit(solution)/shard_map/conv_general_dilated | solution.py:95
  591.8 6.8 %copy.95 = f32[4,64,4096]{2,1,0:T(8,128)} copy(f32[4,64,4096]{1,2,0:T(8,128)} %bitcast.176) | data formatting | bytes 8388608 | tf_op jit(solution)/shard_map/reshape | solution.py:103
  612.5 10.4 %collective-permute-done.16 = bf16[1,1,64,4096]{3,2,1,0:T(8,128)(2,1)S(1)} collective-permute-done((bf16[1,1,64,4096]{3,2,1,0:T(8,128)(2,1)S(1)}, bf16[1,1,64,4096]{3,2,1,0:T(8,128)(2,1)S(1)}, u32[]{:S(2)}, u32[]{:S(2)}) %collective-permute-start.16) | collective-permute-done | bytes 524320 | tf_op jit(solution)/shard_map/ppermute | solution.py:18
  629.6 6.0 select_convert_fusion
  (192 shorter events, 209.6 us)
Async XLA Ops:
  0.0 200.3 %copy-start = (bf16[27,64,64]{2,1,0:T(8,128)(2,1)S(1)}, bf16[27,64,64]{2,1,0:T(8,128)(2,1)}, u32[]{:S(2)}) copy-start(bf16[27,64,64]{2,1,0:T(8,128)(2,1)} %param.20) | copy-start | bytes 663556
  0.0 30.2 %copy-start.6 = (s32[6,6]{1,0:T(8,128)S(1)}, s32[6,6]{1,0:T(8,128)}, u32[]{:S(2)}) copy-start(s32[6,6]{1,0:T(8,128)} %param.19) | copy-start | bytes 436
  0.0 30.8 %copy-start.7 = (s32[6]{0:T(128)S(1)}, s32[6]{0:T(128)}, u32[]{:S(2)}) copy-start(s32[6]{0:T(128)} %param.18) | copy-start | bytes 76
  0.0 37.3 %collective-permute-start.6 = (s32[1,6]{1,0:T(1,128)}, s32[1,6]{1,0:T(1,128)S(1)}, u32[]{:S(2)}, u32[]{:S(2)}) collective-permute-start(s32[1,6]{1,0:T(1,128)} %bitcast.213), channel_id=1, source_target_pairs={{0,1},{1,2},{2,3},{3,4},{4,5},{5,6},{6,7},{7,8},{8,9},{9,10},{10,1... | collective-permute-start | bytes 80 | tf_op jit(solution)/shard_map/ppermute | solution.py:18
  3.2 35.6 %collective-permute-start.7 = (s32[1,6]{1,0:T(1,128)}, s32[1,6]{1,0:T(1,128)S(1)}, u32[]{:S(2)}, u32[]{:S(2)}) collective-permute-start(s32[1,6]{1,0:T(1,128)} %bitcast.214), channel_id=1, source_target_pairs={{1,0},{2,1},{3,2},{4,3},{5,4},{6,5},{7,6},{8,7},{9,8},{10,9},{11,1... | collective-permute-start | bytes 80 | tf_op jit(solution)/shard_map/ppermute | solution.py:19
  14.6 32.6 %collective-permute-start = (bf16[6,1,64,256]{2,3,0,1:T(8,128)(2,1)S(1)}, bf16[6,1,64,256]{2,3,0,1:T(8,128)(2,1)}, u32[]{:S(2)}, u32[]{:S(2)}) collective-permute-start(bf16[6,1,64,256]{2,3,0,1:T(8,128)(2,1)S(1)} %bitcast.195), channel_id=1, source_target_pairs={{0,16},{16,32},{32,48},{48,64},{64,80},{80,96},{96,112},{1,17},{17... | collective-permute-start | bytes 589832 | tf_op jit(solution)/shard_map/ppermute | solution.py:18
  18.6 24.7 %collective-permute-start.1 = (bf16[6,1,64,256]{2,3,0,1:T(8,128)(2,1)S(1)}, bf16[6,1,64,256]{2,3,0,1:T(8,128)(2,1)}, u32[]{:S(2)}, u32[]{:S(2)}) collective-permute-start(bf16[6,1,64,256]{2,3,0,1:T(8,128)(2,1)S(1)} %bitcast.197), channel_id=1, source_target_pairs={{0,1},{1,2},{2,3},{3,4},{4,5},{5,6},{6,7},{7,8},{8,9},{9,10},{10,1... | collective-permute-start | bytes 589832 | tf_op jit(solution)/shard_map/ppermute | solution.py:18
  23.8 28.1 %collective-permute-start.2 = (bf16[6,1,64,256]{2,3,0,1:T(8,128)(2,1)}, bf16[6,1,64,256]{2,3,0,1:T(8,128)(2,1)}, u32[]{:S(2)}, u32[]{:S(2)}) collective-permute-start(bf16[6,1,64,256]{2,3,0,1:T(8,128)(2,1)} %bitcast.21), channel_id=1, source_target_pairs={{1,0},{2,1},{3,2},{4,3},{5,4},{6,5},{7,6},{8,7},{9,8},{10,9},{11,1... | collective-permute-start | bytes 589832 | tf_op jit(solution)/shard_map/ppermute | solution.py:19
  37.3 22.8 %collective-permute-start.3 = (bf16[6,1,64,256]{2,3,0,1:T(8,128)(2,1)}, bf16[6,1,64,256]{2,3,0,1:T(8,128)(2,1)}, u32[]{:S(2)}, u32[]{:S(2)}) collective-permute-start(bf16[6,1,64,256]{2,3,0,1:T(8,128)(2,1)} %bitcast.26), channel_id=1, source_target_pairs={{16,0},{32,16},{48,32},{64,48},{80,64},{96,80},{112,96},{17,1},{33... | collective-permute-start | bytes 589832 | tf_op jit(solution)/shard_map/ppermute | solution.py:19
  43.3 66.9 %copy-start.13 = (s32[4]{0:T(128)}, s32[4]{0:T(128)S(1)}, u32[]{:S(2)}) copy-start(s32[4]{0:T(128)S(1)} %select_reduce_fusion) | copy-start | bytes 52
  100.4 22.5 %collective-permute-start.4 = (bf16[1,1,64,5832]{3,2,1,0:T(8,128)(2,1)}, bf16[1,1,64,5832]{3,2,1,0:T(8,128)(2,1)S(1)}, u32[]{:S(2)}, u32[]{:S(2)}) collective-permute-start(bf16[1,1,64,5832]{3,2,1,0:T(8,128)(2,1)} %copy.71), channel_id=1, source_target_pairs={{0,1},{1,2},{2,3},{3,4},{4,5},{5,6},{6,7},{7,8},{8,9},{9,10},{10,1... | collective-permute-start | bytes 2239496 | tf_op jit(solution)/shard_map/ppermute | solution.py:18
  107.9 23.1 %collective-permute-start.5 = (bf16[1,1,64,5832]{3,2,1,0:T(8,128)(2,1)S(1)}, bf16[1,1,64,5832]{3,2,1,0:T(8,128)(2,1)}, u32[]{:S(2)}, u32[]{:S(2)}) collective-permute-start(bf16[1,1,64,5832]{3,2,1,0:T(8,128)(2,1)S(1)} %copy.73), channel_id=1, source_target_pairs={{1,0},{2,1},{3,2},{4,3},{5,4},{6,5},{7,6},{8,7},{9,8},{10,9},{11,1... | collective-permute-start | bytes 2239496 | tf_op jit(solution)/shard_map/ppermute | solution.py:19
  187.5 4.7 copy-start.3
  192.1 8.2 %copy-start.14 = (pred[32,3]{0,1:T(4,128)(4,1)S(1)}, pred[32,3]{0,1:T(4,128)(4,1)}, u32[]{:S(2)}) copy-start(pred[32,3]{0,1:T(4,128)(4,1)} %constant.122) | copy-start | bytes 292
  281.9 6.8 %copy-start.10 = (f32[64]{0:T(128)S(1)}, f32[64]{0:T(128)}, u32[]{:S(2)}) copy-start(f32[64]{0:T(128)} %param.21) | copy-start | bytes 772
  294.1 10.5 %copy-start.8 = (s32[6]{0:T(128)S(1)}, s32[6]{0:T(128)}, u32[]{:S(2)}) copy-start(s32[6]{0:T(128)} %get-tuple-element.25) | copy-start | bytes 76
  298.8 16.2 %collective-permute-start.8 = (bf16[1,1,64,4096]{3,2,1,0:T(8,128)(2,1)S(1)}, bf16[1,1,64,4096]{3,2,1,0:T(8,128)(2,1)S(1)}, u32[]{:S(2)}, u32[]{:S(2)}) collective-permute-start(bf16[1,1,64,4096]{3,2,1,0:T(8,128)(2,1)S(1)} %get-tuple-element.44), channel_id=1, source_target_pairs={{0,1},{1,2},{2,3},{3,4},{4,5},{5,6},{6,7},{7,8},{8,9},{9,10},{10,1... | collective-permute-start | bytes 1572872 | tf_op jit(solution)/shard_map/ppermute | solution.py:18
  300.7 18.4 %collective-permute-start.9 = (bf16[1,1,64,4096]{3,2,1,0:T(8,128)(2,1)S(1)}, bf16[1,1,64,4096]{3,2,1,0:T(8,128)(2,1)S(1)}, u32[]{:S(2)}, u32[]{:S(2)}) collective-permute-start(bf16[1,1,64,4096]{3,2,1,0:T(8,128)(2,1)S(1)} %get-tuple-element.45), channel_id=1, source_target_pairs={{1,0},{2,1},{3,2},{4,3},{5,4},{6,5},{7,6},{8,7},{9,8},{10,9},{11,1... | collective-permute-start | bytes 1572872 | tf_op jit(solution)/shard_map/ppermute | solution.py:19
  340.9 14.6 %collective-permute-start.10 = (bf16[6,1,64,256]{2,3,0,1:T(8,128)(2,1)S(1)}, bf16[6,1,64,256]{2,3,0,1:T(8,128)(2,1)}, u32[]{:S(2)}, u32[]{:S(2)}) collective-permute-start(bf16[6,1,64,256]{2,3,0,1:T(8,128)(2,1)S(1)} %bitcast.203), channel_id=1, source_target_pairs={{0,16},{16,32},{32,48},{48,64},{64,80},{80,96},{96,112},{1,17},{17... | collective-permute-start | bytes 589832 | tf_op jit(solution)/shard_map/ppermute | solution.py:18
  343.3 16.7 %collective-permute-start.11 = (bf16[6,1,64,256]{2,3,0,1:T(8,128)(2,1)S(1)}, bf16[6,1,64,256]{2,3,0,1:T(8,128)(2,1)}, u32[]{:S(2)}, u32[]{:S(2)}) collective-permute-start(bf16[6,1,64,256]{2,3,0,1:T(8,128)(2,1)S(1)} %bitcast.201), channel_id=1, source_target_pairs={{0,1},{1,2},{2,3},{3,4},{4,5},{5,6},{6,7},{7,8},{8,9},{9,10},{10,1... | collective-permute-start | bytes 589832 | tf_op jit(solution)/shard_map/ppermute | solution.py:18
  345.2 20.0 %collective-permute-start.12 = (bf16[6,1,64,256]{2,3,0,1:T(8,128)(2,1)S(1)}, bf16[6,1,64,256]{2,3,0,1:T(8,128)(2,1)}, u32[]{:S(2)}, u32[]{:S(2)}) collective-permute-start(bf16[6,1,64,256]{2,3,0,1:T(8,128)(2,1)S(1)} %bitcast.199), channel_id=1, source_target_pairs={{1,0},{2,1},{3,2},{4,3},{5,4},{6,5},{7,6},{8,7},{9,8},{10,9},{11,1... | collective-permute-start | bytes 589832 | tf_op jit(solution)/shard_map/ppermute | solution.py:19
  354.2 17.9 %collective-permute-start.13 = (bf16[6,1,64,256]{2,3,0,1:T(8,128)(2,1)}, bf16[6,1,64,256]{2,3,0,1:T(8,128)(2,1)}, u32[]{:S(2)}, u32[]{:S(2)}) collective-permute-start(bf16[6,1,64,256]{2,3,0,1:T(8,128)(2,1)} %bitcast.71), channel_id=1, source_target_pairs={{16,0},{32,16},{48,32},{64,48},{80,64},{96,80},{112,96},{17,1},{33... | collective-permute-start | bytes 589832 | tf_op jit(solution)/shard_map/ppermute | solution.py:19
  412.5 21.1 %collective-permute-start.14 = (bf16[1,1,64,5832]{3,2,1,0:T(8,128)(2,1)}, bf16[1,1,64,5832]{3,2,1,0:T(8,128)(2,1)S(1)}, u32[]{:S(2)}, u32[]{:S(2)}) collective-permute-start(bf16[1,1,64,5832]{3,2,1,0:T(8,128)(2,1)} %copy.87), channel_id=1, source_target_pairs={{0,1},{1,2},{2,3},{3,4},{4,5},{5,6},{6,7},{7,8},{8,9},{9,10},{10,1... | collective-permute-start | bytes 2239496 | tf_op jit(solution)/shard_map/ppermute | solution.py:18
  417.9 23.1 %collective-permute-start.15 = (bf16[1,1,64,5832]{3,2,1,0:T(8,128)(2,1)S(1)}, bf16[1,1,64,5832]{3,2,1,0:T(8,128)(2,1)}, u32[]{:S(2)}, u32[]{:S(2)}) collective-permute-start(bf16[1,1,64,5832]{3,2,1,0:T(8,128)(2,1)S(1)} %copy.89), channel_id=1, source_target_pairs={{1,0},{2,1},{3,2},{4,3},{5,4},{6,5},{7,6},{8,7},{9,8},{10,9},{11,1... | collective-permute-start | bytes 2239496 | tf_op jit(solution)/shard_map/ppermute | solution.py:19
  502.1 8.2 %copy-start.12 = (bf16[27,64,64]{2,1,0:T(8,128)(2,1)S(1)}, bf16[27,64,64]{2,1,0:T(8,128)(2,1)}, u32[]{:S(2)}) copy-start(bf16[27,64,64]{2,1,0:T(8,128)(2,1)} %param.22) | copy-start | bytes 663556
  502.1 8.2 %copy-start.15 = (pred[32,3]{0,1:T(4,128)(4,1)S(1)}, pred[32,3]{0,1:T(4,128)(4,1)}, u32[]{:S(2)}) copy-start(pred[32,3]{0,1:T(4,128)(4,1)} %constant.122) | copy-start | bytes 292
  591.8 6.8 %copy-start.11 = (f32[64]{0:T(128)S(1)}, f32[64]{0:T(128)}, u32[]{:S(2)}) copy-start(f32[64]{0:T(128)} %param.23) | copy-start | bytes 772
  606.6 20.4 %copy-start.5 = (bf16[8,64,4096]{2,1,0:T(8,128)(2,1)}, bf16[8,64,4096]{2,1,0:T(8,128)(2,1)S(1)}, u32[]{:S(2)}) copy-start(bf16[8,64,4096]{2,1,0:T(8,128)(2,1)S(1)} %broadcast_select_fusion.5) | copy-start | bytes 12582916
  606.6 23.0 %copy-start.9 = (pred[6]{0:T(512)(128)(4,1)S(1)}, pred[6]{0:T(512)(128)(4,1)}, u32[]{:S(2)}) copy-start(pred[6]{0:T(512)(128)(4,1)} %get-tuple-element.50) | copy-start | bytes 22
  606.7 16.3 %collective-permute-start.16 = (bf16[1,1,64,4096]{3,2,1,0:T(8,128)(2,1)S(1)}, bf16[1,1,64,4096]{3,2,1,0:T(8,128)(2,1)S(1)}, u32[]{:S(2)}, u32[]{:S(2)}) collective-permute-start(bf16[1,1,64,4096]{3,2,1,0:T(8,128)(2,1)S(1)} %get-tuple-element.42), channel_id=1, source_target_pairs={{0,1},{1,2},{2,3},{3,4},{4,5},{5,6},{6,7},{7,8},{8,9},{9,10},{10,1... | collective-permute-start | bytes 1572872 | tf_op jit(solution)/shard_map/ppermute | solution.py:18
  608.6 18.4 %collective-permute-start.17 = (bf16[1,1,64,4096]{3,2,1,0:T(8,128)(2,1)S(1)}, bf16[1,1,64,4096]{3,2,1,0:T(8,128)(2,1)S(1)}, u32[]{:S(2)}, u32[]{:S(2)}) collective-permute-start(bf16[1,1,64,4096]{3,2,1,0:T(8,128)(2,1)S(1)} %get-tuple-element.43), channel_id=1, source_target_pairs={{1,0},{2,1},{3,2},{4,3},{5,4},{6,5},{7,6},{8,7},{9,8},{10,9},{11,1... | collective-permute-start | bytes 1572872 | tf_op jit(solution)/shard_map/ppermute | solution.py:19
  629.6 6.0 copy-start.1
  (2 other events, 6.6 us)
where the time goes:
time: 648 us; the launch traced here: 636 us
  local copies, waits for them, and re-layouts  291 us (45%)
  other arithmetic  122 us (19%)
  matrix products  103 us (16%)
  waiting for transfers between devices  66.8 us (10%)
  starting transfers between devices  52.3 us (8%)
    conv_general_dilated x2, matrix products, convolve(): lax.conv_general_dilated(cubes, kernel, (1, 1, 1), 'VALID', dimension_num...  103 us
    conv_general_dilated x8, local copies, waits for them, and re-layouts, convolve(): lax.conv_general_dilated(cubes, kernel, (1, 1, 1), 'VALID', dimension_num...  68.4 us
    ppermute x9, waiting for transfers between devices, with_halo(): before = lax.ppermute(last, axis, up)  46.1 us
    select_n x2, local copies, waits for them, and re-layouts, run_held(): held_bricks = jnp.take(candidates, hold_source, axis=0)  45.2 us
    reshape x2, local copies, waits for them, and re-layouts, padded_of(): return full.reshape(bricks, channels, padded_side ** 3)  32.3 us
    ppermute x9, starting transfers between devices, with_halo(): before = lax.ppermute(last, axis, up)  28.6 us
    ppermute x9, starting transfers between devices, with_halo(): after = lax.ppermute(leading, axis, down)  23.8 us
    concatenate x2, other arithmetic, padded_of(): full = jnp.concatenate([lower_x, core, upper_x], axis=2)  22 us
  transfers between devices with their start and end apart: 18, of which 8 were waited for; matrix products, arithmetic and copies ran while one was open for 11% of the time, Pallas kernels for 0%

commit v1 on v0

v1 whole, which is shorter than its diff:
```python
import functools

import jax
import jax.numpy as jnp
from jax import lax
from jax.experimental import pallas as pl
from jax.experimental.pallas import tpu as pltpu
from jax.sharding import PartitionSpec as P

EDGE = 16
SLAB = EDGE * EDGE
HALF = SLAB // 2
MESH = pl.DeviceIdType.MESH
VMEM = pltpu.VMEM
LIMIT = 60 * 2**20


def lanes(rows):
    return lax.broadcasted_iota(jnp.int32, (rows, HALF), 1)


def turn(values, shift):
    shift = shift % HALF
    return values if shift == 0 else pltpu.roll(values, shift, axis=1)


def gather_row(plane, slab_half, x, source_lane):
    place = (x % 8) * EDGE
    lane = lanes(plane.shape[0])
    inside = (lane >= place) & (lane < place + EDGE)
    return jnp.where(inside, turn(slab_half, place - source_lane), plane)


def exchange_body(extract, source, *refs):
    if extract:
        halo_x, halo_y, planes_out, staged, planes, load_sem, send_sem, recv_sem, keep_sem = refs
    else:
        planes, halo_x, halo_y, send_sem, recv_sem = refs
    channels = source.shape[1]
    bricks = source.shape[0]
    n_x, n_y = lax.axis_size("gx"), lax.axis_size("yz")
    gx, yz = lax.axis_index("gx"), lax.axis_index("yz")
    x_up = (lax.rem(gx + 1, n_x), yz)
    x_down = (lax.rem(gx + n_x - 1, n_x), yz)
    y_up = (gx, lax.rem(yz + 1, n_y))
    y_down = (gx, lax.rem(yz + n_y - 1, n_y))

    if extract:
        load = pltpu.make_async_copy(source, staged, load_sem)
        load.start()
    barrier = pltpu.get_barrier_semaphore()
    for other in (x_up, x_down, y_up, y_down):
        pl.semaphore_signal(barrier, inc=1, device_id=other, device_id_type=MESH)
    pl.semaphore_wait(barrier, 4)

    def send(index, src, dst, other):
        copy = pltpu.make_async_remote_copy(
            src_ref=src,
            dst_ref=dst,
            send_sem=send_sem.at[index],
            recv_sem=recv_sem.at[index],
            device_id=other,
            device_id_type=MESH,
        )
        copy.start()
        return copy

    copies = [
        send(0, source.at[:, :, pl.ds((EDGE - 1) * SLAB, SLAB)], halo_x.at[0], x_up),
        send(1, source.at[:, :, pl.ds(0, SLAB)], halo_x.at[1], x_down),
    ]
    if extract:
        load.wait()

        def one_brick(b, carry):
            for half in range(2):
                low = jnp.zeros((channels, HALF), staged.dtype)
                high = low
                for x in range(half * 8, half * 8 + 8):
                    low = gather_row(low, staged[b, :, x * SLAB : x * SLAB + HALF], x, 0)
                    high = gather_row(
                        high, staged[b, :, x * SLAB + HALF : (x + 1) * SLAB], x, HALF - EDGE
                    )
                planes[0, b, :, half * HALF : (half + 1) * HALF] = low
                planes[1, b, :, half * HALF : (half + 1) * HALF] = high
            return carry

        lax.fori_loop(0, bricks, one_brick, 0)
    copies.append(send(2, planes.at[1], halo_y.at[0], y_up))
    copies.append(send(3, planes.at[0], halo_y.at[1], y_down))
    if extract:
        keep = pltpu.make_async_copy(planes, planes_out, keep_sem)
        keep.start()
        keep.wait()
    for copy in copies:
        copy.wait()


def first_exchange(features):
    bricks, channels, _ = features.shape
    plane = jax.ShapeDtypeStruct((2, bricks, channels, SLAB), features.dtype)
    anywhere = pl.BlockSpec(memory_space=pl.ANY)
    return pl.pallas_call(
        functools.partial(exchange_body, True),
        out_shape=(plane, plane, plane),
        in_specs=[anywhere],
        out_specs=(anywhere, anywhere, anywhere),
        scratch_shapes=[
            VMEM(features.shape, features.dtype),
            VMEM(plane.shape, plane.dtype),
            pltpu.SemaphoreType.DMA,
            pltpu.SemaphoreType.DMA((4,)),
            pltpu.SemaphoreType.DMA((4,)),
            pltpu.SemaphoreType.DMA,
        ],
        compiler_params=pltpu.CompilerParams(
            collective_id=0, has_side_effects=True, vmem_limit_bytes=LIMIT
        ),
        name="exchange_features",
    )(features)


def second_exchange(hidden, planes):
    plane = jax.ShapeDtypeStruct(planes.shape, planes.dtype)
    anywhere = pl.BlockSpec(memory_space=pl.ANY)
    return pl.pallas_call(
        functools.partial(exchange_body, False),
        out_shape=(plane, plane),
        in_specs=[anywhere, anywhere],
        out_specs=(anywhere, anywhere),
        scratch_shapes=[
            pltpu.SemaphoreType.DMA((4,)),
            pltpu.SemaphoreType.DMA((4,)),
        ],
        compiler_params=pltpu.CompilerParams(
            collective_id=1, has_side_effects=True, vmem_limit_bytes=LIMIT
        ),
        name="exchange_hidden",
    )(hidden, planes)


def conv_body(
    last, state, neighbor, values, halo_x, halo_y, own_y, weights, bias, *refs
):
    if last:
        features, out, stacked, matrix, bias_column = refs
    else:
        out, planes_out, stacked, matrix, bias_column = refs
    b = pl.program_id(0)
    bricks, channels = values.shape[0], values.shape[1]
    kind = values.dtype
    lane = lanes(channels)
    z = lane % EDGE
    zero = jnp.zeros((channels, HALF), kind)

    @pl.when(b == 0)
    def _():
        for dy in range(3):
            blocks = [weights[9 * (j // 3) + 3 * dy + j % 3] for j in range(9)]
            rows = pl.ds(dy * channels, channels)
            for pair in range(4):
                matrix[rows, pair * 2 * channels : (pair + 1) * 2 * channels] = jnp.concatenate(
                    blocks[2 * pair : 2 * pair + 2], axis=1
                )
            matrix[rows, 8 * channels : 9 * channels] = blocks[8]
        row = lax.broadcasted_iota(jnp.int32, (channels, channels), 0)
        column = lax.broadcasted_iota(jnp.int32, (channels, channels), 1)
        wide = jnp.broadcast_to(bias[...], (channels, channels))
        one = jnp.sum(jnp.where(row == column, wide, 0.0), axis=1, keepdims=True)
        bias_column[...] = jnp.broadcast_to(one, (channels, HALF))

    def face(index, own, across):
        k = neighbor[b, index]
        here = jnp.clip(k, 0, bricks - 1)
        there = jnp.clip(k - bricks, 0, bricks - 1)
        picked = jnp.where(k < bricks, own(here), across[index % 2, there])
        return jnp.where(k >= 0, picked, jnp.zeros_like(picked))

    def z_shifted(half, below, above):
        down = jnp.where(z == 0, below, turn(half, 1))
        up = jnp.where(z == EDGE - 1, above, turn(half, -1))
        return down, half, up

    def compute():
        def y_face(index):
            plane = face(index, lambda k: own_y[1 - index % 2, k], halo_y)
            a, c = plane[:, :HALF], plane[:, HALF:]
            ra, rc = turn(a, EDGE), turn(c, EDGE)
            before = (jnp.where(lane < EDGE, zero, ra), jnp.where(lane < EDGE, ra, rc))
            ra, rc = turn(a, -EDGE), turn(c, -EDGE)
            edge = lane >= HALF - EDGE
            after = (jnp.where(edge, rc, ra), jnp.where(edge, zero, rc))
            blocks = []
            for left, right in (before, (a, c), after):
                for l, r in zip(z_shifted(left, zero, zero), z_shifted(right, zero, zero)):
                    blocks.append(jnp.concatenate([l, r], axis=1))
            tall = jnp.concatenate(blocks, axis=0)
            dy = 2 * (index % 2)
            return jnp.dot(
                matrix[dy * channels : (dy + 1) * channels, :],
                tall,
                preferred_element_type=jnp.float32,
            )

        low_y, high_y = y_face(2), y_face(3)

        def put(x, a_shifts, c_shifts):
            for dz in range(3):
                rows = pl.ds(dz * channels, channels)
                stacked[x + 1, rows, :HALF] = a_shifts[dz]
                stacked[x + 1, rows, HALF:] = c_shifts[dz]

        for x, index in ((-1, 0), (EDGE, 1)):
            first = (EDGE - 1) * SLAB if index == 0 else 0
            slab = face(index, lambda k, first=first: values[k, :, first : first + SLAB], halo_x)
            put(x, z_shifted(slab[:, :HALF], zero, zero), z_shifted(slab[:, HALF:], zero, zero))

        def z_neighbor(index):
            k = neighbor[b, index]
            return k >= 0, jnp.clip(jnp.where(k >= bricks, k - bricks, k), 0, bricks - 1)

        has_below, below = z_neighbor(4)
        has_above, above = z_neighbor(5)
        for x in range(EDGE):
            shifts = []
            for half in range(2):
                first = x * SLAB + half * HALF
                low = turn(values[below, :, first : first + HALF], 1 - EDGE)
                high = turn(values[above, :, first : first + HALF], EDGE - 1)
                shifts.append(
                    z_shifted(
                        values[b, :, first : first + HALF],
                        jnp.where(has_below, low, zero),
                        jnp.where(has_above, high, zero),
                    )
                )
            put(x, *shifts)

        if not last:
            low_planes, high_planes = [zero, zero], [zero, zero]
        for x in range(EDGE):
            taps = stacked[x : x + 3].reshape(9 * channels, SLAB)
            sums = jnp.dot(matrix[...], taps, preferred_element_type=jnp.float32)
            before, middle, after = (
                sums[i * channels : (i + 1) * channels] for i in range(3)
            )
            quarter = x // 8
            place = (x % 8) * EDGE
            low = turn(low_y[:, quarter * HALF : (quarter + 1) * HALF], -place)
            high = turn(high_y[:, quarter * HALF : (quarter + 1) * HALF], HALF - EDGE - place)
            ra, rc = turn(before[:, :HALF], EDGE), turn(before[:, HALF:], EDGE)
            first = (jnp.where(lane < EDGE, low, ra), jnp.where(lane < EDGE, ra, rc))
            ra, rc = turn(after[:, :HALF], -EDGE), turn(after[:, HALF:], -EDGE)
            edge = lane >= HALF - EDGE
            second = (jnp.where(edge, rc, ra), jnp.where(edge, high, rc))
            for half in range(2):
                span = slice(x * SLAB + half * HALF, x * SLAB + (half + 1) * HALF)
                total = middle[:, half * HALF : (half + 1) * HALF] + first[half]
                total = total + second[half] + bias_column[...]
                if last:
                    branch = total.astype(kind).astype(jnp.float32)
                    total = features[0, :, span].astype(jnp.float32) + branch
                done = jnp.maximum(total, 0.0).astype(kind)
                out[0, :, span] = done
                if not last and half == 0:
                    low_planes[quarter] = gather_row(low_planes[quarter], done, x, 0)
                elif not last:
                    high_planes[quarter] = gather_row(high_planes[quarter], done, x, HALF - EDGE)
        if not last:
            for quarter in range(2):
                span = slice(quarter * HALF, (quarter + 1) * HALF)
                planes_out[0, 0, :, span] = low_planes[quarter]
                planes_out[1, 0, :, span] = high_planes[quarter]

    live = state[b] >= 0

    @pl.when(live)
    def _():
        compute()

    @pl.when(jnp.logical_not(live))
    def _():
        out[...] = jnp.zeros_like(out)
        if not last:
            planes_out[...] = jnp.zeros_like(planes_out)


def conv(last, state, neighbor, values, halo_x, halo_y, own_y, weights, bias, features=None):
    bricks, channels, voxels = values.shape
    kind = values.dtype
    whole = pl.BlockSpec(memory_space=VMEM)
    scalar = pl.BlockSpec(memory_space=pltpu.SMEM)
    brick = pl.BlockSpec((1, channels, voxels), lambda b: (b, 0, 0))
    plane = pl.BlockSpec((2, 1, channels, SLAB), lambda b: (0, b, 0, 0))
    args = [state, neighbor, values, halo_x, halo_y, own_y, weights, bias.reshape(1, channels)]
    in_specs = [scalar, scalar] + [whole] * 6
    out_shape = jax.ShapeDtypeStruct(values.shape, kind)
    out_specs = brick
    if last:
        args.append(features)
        in_specs.append(brick)
    else:
        out_shape = (out_shape, jax.ShapeDtypeStruct((2, bricks, channels, SLAB), kind))
        out_specs = (brick, plane)
    return pl.pallas_call(
        functools.partial(conv_body, last),
        grid=(bricks,),
        out_shape=out_shape,
        in_specs=in_specs,
        out_specs=out_specs,
        scratch_shapes=[
            VMEM((EDGE + 2, 3 * channels, SLAB), kind),
            VMEM((3 * channels, 9 * channels), kind),
            VMEM((channels, HALF), jnp.float32),
        ],
        compiler_params=pltpu.CompilerParams(vmem_limit_bytes=LIMIT),
        name="second_conv" if last else "first_conv",
    )(*args)


def per_device(features, brick_state, neighbor, w_first, b_first, w_second, b_second):
    halo_x, halo_y, own_y = first_exchange(features)
    hidden, planes = conv(
        False, brick_state, neighbor, features, halo_x, halo_y, own_y, w_first, b_first
    )
    halo_x, halo_y = second_exchange(hidden, planes)
    return conv(
        True, brick_state, neighbor, hidden, halo_x, halo_y, planes, w_second, b_second, features
    )


def solution(mesh):
    in_specs = (
        P(("gx", "yz"), None, None),
        P(("gx", "yz")),
        P(("gx", "yz"), None),
        P(),
        P(),
        P(),
        P(),
    )
    out_specs = P(("gx", "yz"), None, None)
    return jax.shard_map(
        per_device, mesh=mesh, in_specs=in_specs, out_specs=out_specs, check_vma=False
    )
```

time: 648 us -> 56.6 us (0.09)
  the two profiles are of different devices: /device:TPU:24 before, /device:TPU:64 now
where the time goes in v1:
time: 56.6 us; the launch traced here: 56.4 us
  Pallas kernels  56.4 us (100%)
    pallas_call x2, Pallas kernels, conv(): pl.pallas_call(functools.partial(conv_body, last), grid=(bricks,), out_sh...  32.7 us
    pallas_call x1, Pallas kernels, first_exchange(): pl.pallas_call(functools.partial(exchange_body, True), out_shape=(plane,...  13.3 us
    pallas_call x1, Pallas kernels, second_exchange(): pl.pallas_call(functools.partial(exchange_body, False), out_shape=(plane,...  10.4 us

profile of v1, /device:TPU:64, one launch (start us, length us, event | category | flops | bytes accessed | tf_op | source)
XLA Modules:
  0.0 56.4 jit_solution(18324254942503747243)
XLA Ops:
  0.0 13.3 %exchange_features.1 = (bf16[2,6,64,256]{3,2,1,0:T(8,128)(2,1)}, bf16[2,6,64,256]{3,2,1,0:T(8,128)(2,1)}, bf16[2,6,64,256]{3,2,1,0:T(8,128)(2,1)}) custom-call(bf16[6,64,4096]{2,1,0:T(8,128)(2,1)} %refs_0_.1), custom_call_target="tpu_custom_call" | custom-call | tf_op jit(solution)/shard_map/exchange_features/pallas_call | solution.py:103
  13.4 18.2 %first_conv.1 = (bf16[6,64,4096]{2,1,0:T(8,128)(2,1)}, bf16[2,6,64,256]{3,2,1,0:T(8,128)(2,1)}) custom-call(s32[6]{0:T(128)} %state.3, s32[6,6]{1,0:T(8,128)} %neighbor.3, bf16[6,64,4096]{2,1,0:T(8,128)(2,1)} %refs_0_.1, bf16[2,6,64,256]{3,2,1,0:T(8,128)(2,1)} %get-tuple-element.12.halo_x, bf16[2,6,64,256]{3,2,1,0:T(8,128)(2,1)} %get-tuple-element.13.halo_y, ...), custom_call_target="tpu_custom_call" | custom-call | tf_op jit(solution)/shard_map/first_conv/pallas_call | solution.py:305
  31.5 10.4 %exchange_hidden.1 = (bf16[2,6,64,256]{3,2,1,0:T(8,128)(2,1)}, bf16[2,6,64,256]{3,2,1,0:T(8,128)(2,1)}) custom-call(bf16[6,64,4096]{2,1,0:T(8,128)(2,1)} %get-tuple-element.15.source.values, bf16[2,6,64,256]{3,2,1,0:T(8,128)(2,1)} %get-tuple-element.16.refs_0_.own_y), custom_call_target="tpu_custom_call" | custom-call | tf_op jit(solution)/shard_map/exchange_hidden/pallas_call | solution.py:126
  41.9 14.5 %second_conv.1 = bf16[6,64,4096]{2,1,0:T(8,128)(2,1)} custom-call(s32[6]{0:T(128)} %state.3, s32[6,6]{1,0:T(8,128)} %neighbor.3, bf16[6,64,4096]{2,1,0:T(8,128)(2,1)} %get-tuple-element.15.source.values, bf16[2,6,64,256]{3,2,1,0:T(8,128)(2,1)} %get-tuple-element.17.halo_x, bf16[2,6,64,256]{3,2,1,0:T(8,128)(2,1)} %get-tuple-element.18.halo_y, ...), custom_call_target="tpu_custom_call" | custom-call | tf_op jit(solution)/shard_map/second_conv/pallas_call | solution.py:305

commit v2 on v0

v2 whole, which is shorter than its diff:
```python
import jax
import jax.numpy as jnp
from jax import lax
from jax.experimental import pallas as pl
from jax.experimental.pallas import tpu as pltpu
from jax.sharding import PartitionSpec as P

EDGE = 16
SLAB = EDGE * EDGE
HALF = SLAB // 2
MESH = pl.DeviceIdType.MESH
VMEM = pltpu.VMEM
LIMIT = 60 * 2**20


def lanes(rows):
    return lax.broadcasted_iota(jnp.int32, (rows, HALF), 1)


def turn(values, shift):
    shift = shift % HALF
    return values if shift == 0 else pltpu.roll(values, shift, axis=1)


def gather_row(plane, slab_half, x, source_lane):
    place = (x % 8) * EDGE
    lane = lanes(plane.shape[0])
    inside = (lane >= place) & (lane < place + EDGE)
    return jnp.where(inside, turn(slab_half, place - source_lane), plane)


def at_x(x):
    return slice(x * SLAB, (x + 1) * SLAB)


def outer_rows(values, b, planes):
    channels = values.shape[1]
    for half in range(2):
        low = jnp.zeros((channels, HALF), values.dtype)
        high = low
        for x in range(half * 8, half * 8 + 8):
            low = gather_row(low, values[b, :, x * SLAB : x * SLAB + HALF], x, 0)
            high = gather_row(high, values[b, :, x * SLAB + HALF : (x + 1) * SLAB], x, HALF - EDGE)
        planes[0, b, :, half * HALF : (half + 1) * HALF] = low
        planes[1, b, :, half * HALF : (half + 1) * HALF] = high


def z_shifted(half, below, above):
    z = lanes(half.shape[0]) % EDGE
    down = jnp.where(z == 0, below, turn(half, 1))
    up = jnp.where(z == EDGE - 1, above, turn(half, -1))
    return down, half, up


def put(stacked, b, x, left, right):
    channels = left[0].shape[0]
    for dz in range(3):
        rows = slice(dz * channels, (dz + 1) * channels)
        stacked[b, x + 1, rows, :HALF] = left[dz]
        stacked[b, x + 1, rows, HALF:] = right[dz]


def stack_brick(values, neighbor, b, stacked):
    bricks, channels = values.shape[0], values.shape[1]
    zero = jnp.zeros((channels, HALF), values.dtype)

    def z_neighbor(index):
        k = neighbor[b, index]
        return k >= 0, jnp.clip(jnp.where(k >= bricks, k - bricks, k), 0, bricks - 1)

    has_below, below = z_neighbor(4)
    has_above, above = z_neighbor(5)
    for x in range(EDGE):
        shifts = []
        for half in range(2):
            span = slice(x * SLAB + half * HALF, x * SLAB + (half + 1) * HALF)
            low = turn(values[below, :, span], 1 - EDGE)
            high = turn(values[above, :, span], EDGE - 1)
            shifts.append(
                z_shifted(
                    values[b, :, span],
                    jnp.where(has_below, low, zero),
                    jnp.where(has_above, high, zero),
                )
            )
        put(stacked, b, x, *shifts)


def conv_brick(values, halo_x, halo_y, own_y, neighbor, b, stacked, matrix, bias, finish):
    bricks, channels = values.shape[0], values.shape[1]
    lane = lanes(channels)
    zero = jnp.zeros((channels, HALF), values.dtype)
    edge = lane >= HALF - EDGE

    def face(index, own, across):
        k = neighbor[b, index]
        here = jnp.clip(k, 0, bricks - 1)
        there = jnp.clip(k - bricks, 0, bricks - 1)
        picked = jnp.where(k < bricks, own(here), across[index % 2, there])
        return jnp.where(k >= 0, picked, jnp.zeros_like(picked))

    def y_face(index):
        plane = face(index, lambda k: own_y[1 - index % 2, k], halo_y)
        a, c = plane[:, :HALF], plane[:, HALF:]
        ra, rc = turn(a, EDGE), turn(c, EDGE)
        before = (jnp.where(lane < EDGE, zero, ra), jnp.where(lane < EDGE, ra, rc))
        ra, rc = turn(a, -EDGE), turn(c, -EDGE)
        after = (jnp.where(edge, rc, ra), jnp.where(edge, zero, rc))
        blocks = []
        for left, right in (before, (a, c), after):
            for l, r in zip(z_shifted(left, zero, zero), z_shifted(right, zero, zero)):
                blocks.append(jnp.concatenate([l, r], axis=1))
        tall = jnp.concatenate(blocks, axis=0)
        dy = 2 * (index % 2)
        rows = matrix[dy * channels : (dy + 1) * channels, :]
        return jnp.dot(rows, tall, preferred_element_type=jnp.float32)

    low_y, high_y = y_face(2), y_face(3)
    for x, index in ((-1, 0), (EDGE, 1)):
        inner = at_x(EDGE - 1 if index == 0 else 0)
        slab = face(index, lambda k, inner=inner: values[k, :, inner], halo_x)
        left = z_shifted(slab[:, :HALF], zero, zero)
        put(stacked, b, x, left, z_shifted(slab[:, HALF:], zero, zero))
    for x in range(EDGE):
        taps = stacked[b, x : x + 3].reshape(9 * channels, SLAB)
        sums = jnp.dot(matrix[...], taps, preferred_element_type=jnp.float32)
        before, middle, after = (sums[i * channels : (i + 1) * channels] for i in range(3))
        plane_half = slice(x // 8 * HALF, (x // 8 + 1) * HALF)
        place = (x % 8) * EDGE
        low = turn(low_y[:, plane_half], -place)
        high = turn(high_y[:, plane_half], HALF - EDGE - place)
        ra, rc = turn(before[:, :HALF], EDGE), turn(before[:, HALF:], EDGE)
        first = (jnp.where(lane < EDGE, low, ra), jnp.where(lane < EDGE, ra, rc))
        ra, rc = turn(after[:, :HALF], -EDGE), turn(after[:, HALF:], -EDGE)
        second = (jnp.where(edge, rc, ra), jnp.where(edge, high, rc))
        for half in range(2):
            total = middle[:, half * HALF : (half + 1) * HALF] + first[half]
            total = total + second[half] + bias[...]
            finish(slice(x * SLAB + half * HALF, x * SLAB + (half + 1) * HALF), total)


def prepare(weights, bias, matrix, column_out):
    channels = weights.shape[1]
    for dy in range(3):
        blocks = [weights[9 * (j // 3) + 3 * dy + j % 3] for j in range(9)]
        rows = slice(dy * channels, (dy + 1) * channels)
        for pair in range(4):
            columns = slice(pair * 2 * channels, (pair + 1) * 2 * channels)
            matrix[rows, columns] = jnp.concatenate(blocks[2 * pair : 2 * pair + 2], axis=1)
        matrix[rows, 8 * channels : 9 * channels] = blocks[8]
    row = lax.broadcasted_iota(jnp.int32, (channels, channels), 0)
    column = lax.broadcasted_iota(jnp.int32, (channels, channels), 1)
    wide = jnp.broadcast_to(bias[...], (channels, channels))
    one = jnp.sum(jnp.where(row == column, wide, 0.0), axis=1, keepdims=True)
    column_out[...] = jnp.broadcast_to(one, (channels, HALF))


def body(
    state, neighbor, features, w_first, b_first, w_second, b_second, out,
    staged, hidden, result, stacked,
    planes_1, halo_x_1, halo_y_1, planes_2, halo_x_2, halo_y_2,
    weights_1, weights_2, matrix_1, matrix_2, bias_1, bias_2,
    load_sem, weight_sem, store_sem, send_sem_1, recv_sem_1, send_sem_2, recv_sem_2,
):
    bricks = staged.shape[0]
    kind = staged.dtype
    n_x, n_y = lax.axis_size("gx"), lax.axis_size("yz")
    gx, yz = lax.axis_index("gx"), lax.axis_index("yz")
    x_up = (lax.rem(gx + 1, n_x), yz)
    x_down = (lax.rem(gx + n_x - 1, n_x), yz)
    y_up = (gx, lax.rem(yz + 1, n_y))
    y_down = (gx, lax.rem(yz + n_y - 1, n_y))
    others = (x_up, x_down, y_up, y_down)

    barrier = pltpu.get_barrier_semaphore()
    for other in others:
        pl.semaphore_signal(barrier, inc=1, device_id=other, device_id_type=MESH)
    load = pltpu.make_async_copy(features, staged, load_sem)
    load.start()
    weight_loads = [
        pltpu.make_async_copy(w_first, weights_1, weight_sem.at[0]),
        pltpu.make_async_copy(w_second, weights_2, weight_sem.at[1]),
    ]
    for copy in weight_loads:
        copy.start()
    pl.semaphore_wait(barrier, 4)

    def remote(src, dst, sems, other):
        return pltpu.make_async_remote_copy(
            src_ref=src,
            dst_ref=dst,
            send_sem=sems[0],
            recv_sem=sems[1],
            device_id=other,
            device_id_type=MESH,
        )

    last = pl.ds((EDGE - 1) * SLAB, SLAB)
    sems_1 = [(send_sem_1.at[i], recv_sem_1.at[i]) for i in range(4)]
    exchange = [
        remote(features.at[:, :, last], halo_x_1.at[0], sems_1[0], x_up),
        remote(features.at[:, :, pl.ds(0, SLAB)], halo_x_1.at[1], sems_1[1], x_down),
        remote(planes_1.at[1], halo_y_1.at[0], sems_1[2], y_up),
        remote(planes_1.at[0], halo_y_1.at[1], sems_1[3], y_down),
    ]
    exchange[0].start()
    exchange[1].start()
    load.wait()

    @pl.loop(0, bricks)
    def _(b):
        outer_rows(staged, b, planes_1)

    exchange[2].start()
    exchange[3].start()
    for copy in weight_loads:
        copy.wait()
    prepare(weights_1, b_first, matrix_1, bias_1)
    prepare(weights_2, b_second, matrix_2, bias_2)

    @pl.loop(0, bricks)
    def _(b):
        stack_brick(staged, neighbor, b, stacked)

    for copy in exchange:
        copy.wait()

    def hidden_copies(b):
        sems = [(send_sem_2.at[i, b], recv_sem_2.at[i, b]) for i in range(4)]
        return [
            remote(hidden.at[b, :, last], halo_x_2.at[0, b], sems[0], x_up),
            remote(hidden.at[b, :, pl.ds(0, SLAB)], halo_x_2.at[1, b], sems[1], x_down),
            remote(planes_2.at[1, b], halo_y_2.at[0, b], sems[2], y_up),
            remote(planes_2.at[0, b], halo_y_2.at[1, b], sems[3], y_down),
        ]

    @pl.loop(0, bricks)
    def _(b):
        live = state[b] >= 0

        def finish(span, total):
            hidden[b, :, span] = jnp.where(live, jnp.maximum(total, 0.0), 0.0).astype(kind)

        conv_brick(
            staged, halo_x_1, halo_y_1, planes_1, neighbor, b, stacked, matrix_1, bias_1, finish
        )
        outer_rows(hidden, b, planes_2)
        for copy in hidden_copies(b):
            copy.start()

    @pl.loop(0, bricks)
    def _(b):
        stack_brick(hidden, neighbor, b, stacked)

    @pl.loop(0, bricks)
    def _(b):
        for copy in hidden_copies(b):
            copy.wait()

    def store(b):
        return pltpu.make_async_copy(result.at[b], out.at[b], store_sem.at[b])

    @pl.loop(0, bricks)
    def _(b):
        live = state[b] >= 0

        def finish(span, total):
            branch = total.astype(kind).astype(jnp.float32)
            summed = staged[b, :, span].astype(jnp.float32) + branch
            result[b, :, span] = jnp.where(live, jnp.maximum(summed, 0.0), 0.0).astype(kind)

        conv_brick(
            hidden, halo_x_2, halo_y_2, planes_2, neighbor, b, stacked, matrix_2, bias_2, finish
        )
        store(b).start()

    @pl.loop(0, bricks)
    def _(b):
        store(b).wait()


def per_device(features, brick_state, neighbor, w_first, b_first, w_second, b_second):
    bricks, channels, _ = features.shape
    kind = features.dtype
    anywhere = pl.BlockSpec(memory_space=pl.ANY)
    whole = pl.BlockSpec(memory_space=VMEM)
    scalar = pl.BlockSpec(memory_space=pltpu.SMEM)
    brick_set = VMEM(features.shape, kind)
    plane_set = VMEM((2, bricks, channels, SLAB), kind)
    matrix = VMEM((3 * channels, 9 * channels), kind)
    column = VMEM((channels, HALF), jnp.float32)
    dma = pltpu.SemaphoreType.DMA
    return pl.pallas_call(
        body,
        out_shape=jax.ShapeDtypeStruct(features.shape, kind),
        in_specs=[scalar, scalar, anywhere, anywhere, whole, anywhere, whole],
        out_specs=anywhere,
        scratch_shapes=[
            brick_set, brick_set, brick_set,
            VMEM((bricks, EDGE + 2, 3 * channels, SLAB), kind),
            *[plane_set] * 6,
            VMEM(w_first.shape, kind), VMEM(w_second.shape, kind),
            matrix, matrix, column, column,
            dma, dma((2,)), dma((bricks,)),
            dma((4,)), dma((4,)), dma((4, bricks)), dma((4, bricks)),
        ],
        compiler_params=pltpu.CompilerParams(
            collective_id=0, has_side_effects=True, vmem_limit_bytes=LIMIT
        ),
        name="residual_pair",
    )(
        brick_state, neighbor, features,
        w_first, b_first.reshape(1, channels), w_second, b_second.reshape(1, channels),
    )


def solution(mesh):
    in_specs = (
        P(("gx", "yz"), None, None),
        P(("gx", "yz")),
        P(("gx", "yz"), None),
        P(),
        P(),
        P(),
        P(),
    )
    out_specs = P(("gx", "yz"), None, None)
    return jax.shard_map(
        per_device, mesh=mesh, in_specs=in_specs, out_specs=out_specs, check_vma=False
    )
```

time: 648 us -> 46.9 us (0.07)
  the two profiles are of different devices: /device:TPU:24 before, /device:TPU:64 now
where the time goes in v2:
time: 46.9 us; the launch traced here: 46.6 us
  Pallas kernels  42.6 us (91%)
  local copies, waits for them, and re-layouts  3.91 us (8%)
    pallas_call x1, Pallas kernels, per_device(): pl.pallas_call(body, out_shape=jax.ShapeDtypeStruct(features.shape, kind)...  42.6 us
    unnamed x1, local copies, waits for them, and re-layouts  3.91 us

profile of v2, /device:TPU:64, one launch (start us, length us, event | category | flops | bytes accessed | tf_op | source)
XLA Modules:
  0.0 46.6 jit_solution(15364692065101499901)
XLA Ops:
  0.0 42.6 %residual_pair.1 = bf16[6,64,4096]{2,1,0:T(8,128)(2,1)} custom-call(s32[6]{0:T(128)} %state.1, s32[6,6]{1,0:T(8,128)} %neighbor.1, bf16[6,64,4096]{2,1,0:T(8,128)(2,1)} %features.1, bf16[27,64,64]{2,1,0:T(8,128)(2,1)} %w_first.1, f32[1,64]{1,0:T(1,128)} %bitcast.2, bf16[27,64,64]{2,1,0:T(8,128)(2,1)} %w_second.1, f32[1,64]{1,0:T(1,128)} %bitcast.3), custom_call_target="tpu_custom_call" | custom-call | tf_op jit(solution)/shard_map/residual_pair/pallas_call | solution.py:293
  42.6 3.9 %copy.9 = bf16[6,64,4096]{2,1,0:T(8,128)(2,1)} copy(bf16[6,64,4096]{2,1,0:T(8,128)(2,1)} %residual_pair.1) | data formatting | bytes 6291456

commit v3 on v2

--- a/solution.py
+++ b/solution.py
@@ -10,7 +10,7 @@
 HALF = SLAB // 2
 MESH = pl.DeviceIdType.MESH
 VMEM = pltpu.VMEM
-LIMIT = 60 * 2**20
+LIMIT = 58 * 2**20
 
 
 def lanes(rows):
@@ -157,10 +157,10 @@
 
 def body(
     state, neighbor, features, w_first, b_first, w_second, b_second, out,
-    staged, hidden, result, stacked,
+    staged, hidden, stacked,
     planes_1, halo_x_1, halo_y_1, planes_2, halo_x_2, halo_y_2,
     weights_1, weights_2, matrix_1, matrix_2, bias_1, bias_2,
-    load_sem, weight_sem, store_sem, send_sem_1, recv_sem_1, send_sem_2, recv_sem_2,
+    load_sem, weight_sem, send_x, recv_x, send_sem_1, recv_sem_1, send_sem_2, recv_sem_2,
 ):
     bricks = staged.shape[0]
     kind = staged.dtype
@@ -175,8 +175,12 @@
     barrier = pltpu.get_barrier_semaphore()
     for other in others:
         pl.semaphore_signal(barrier, inc=1, device_id=other, device_id_type=MESH)
-    load = pltpu.make_async_copy(features, staged, load_sem)
-    load.start()
+
+    def load(b):
+        return pltpu.make_async_copy(features.at[b], staged.at[b], load_sem.at[b])
+
+    for b in range(bricks):
+        load(b).start()
     weight_loads = [
         pltpu.make_async_copy(w_first, weights_1, weight_sem.at[0]),
         pltpu.make_async_copy(w_second, weights_2, weight_sem.at[1]),
@@ -196,23 +200,30 @@
         )
 
     last = pl.ds((EDGE - 1) * SLAB, SLAB)
-    sems_1 = [(send_sem_1.at[i], recv_sem_1.at[i]) for i in range(4)]
-    exchange = [
-        remote(features.at[:, :, last], halo_x_1.at[0], sems_1[0], x_up),
-        remote(features.at[:, :, pl.ds(0, SLAB)], halo_x_1.at[1], sems_1[1], x_down),
-        remote(planes_1.at[1], halo_y_1.at[0], sems_1[2], y_up),
-        remote(planes_1.at[0], halo_y_1.at[1], sems_1[3], y_down),
+    across_x = [
+        remote(features.at[:, :, last], halo_x_1.at[0], (send_x.at[0], recv_x.at[0]), x_up),
+        remote(
+            features.at[:, :, pl.ds(0, SLAB)], halo_x_1.at[1], (send_x.at[1], recv_x.at[1]), x_down
+        ),
     ]
-    exchange[0].start()
-    exchange[1].start()
-    load.wait()
-
-    @pl.loop(0, bricks)
-    def _(b):
+
+    def across_y(b):
+        sems = [(send_sem_1.at[i, b], recv_sem_1.at[i, b]) for i in range(2)]
+        return [
+            remote(planes_1.at[1, b], halo_y_1.at[0, b], sems[0], y_up),
+            remote(planes_1.at[0, b], halo_y_1.at[1, b], sems[1], y_down),
+        ]
+
+    for copy in across_x:
+        copy.start()
+
+    @pl.loop(0, bricks)
+    def _(b):
+        load(b).wait()
         outer_rows(staged, b, planes_1)
-
-    exchange[2].start()
-    exchange[3].start()
+        for copy in across_y(b):
+            copy.start()
+
     for copy in weight_loads:
         copy.wait()
     prepare(weights_1, b_first, matrix_1, bias_1)
@@ -222,8 +233,13 @@
     def _(b):
         stack_brick(staged, neighbor, b, stacked)
 
-    for copy in exchange:
+    for copy in across_x:
         copy.wait()
+
+    @pl.loop(0, bricks)
+    def _(b):
+        for copy in across_y(b):
+            copy.wait()
 
     def hidden_copies(b):
         sems = [(send_sem_2.at[i, b], recv_sem_2.at[i, b]) for i in range(4)]
@@ -257,9 +273,6 @@
         for copy in hidden_copies(b):
             copy.wait()
 
-    def store(b):
-        return pltpu.make_async_copy(result.at[b], out.at[b], store_sem.at[b])
-
     @pl.loop(0, bricks)
     def _(b):
         live = state[b] >= 0
@@ -267,16 +280,21 @@
         def finish(span, total):
             branch = total.astype(kind).astype(jnp.float32)
             summed = staged[b, :, span].astype(jnp.float32) + branch
-            result[b, :, span] = jnp.where(live, jnp.maximum(summed, 0.0), 0.0).astype(kind)
+            out[b, :, span] = jnp.where(live, jnp.maximum(summed, 0.0), 0.0).astype(kind)
 
         conv_brick(
             hidden, halo_x_2, halo_y_2, planes_2, neighbor, b, stacked, matrix_2, bias_2, finish
         )
-        store(b).start()
-
-    @pl.loop(0, bricks)
-    def _(b):
-        store(b).wait()
+
+
+def store_body(blocks, out, sem):
+    copies = [
+        pltpu.make_async_copy(blocks.at[b], out.at[b], sem.at[b]) for b in range(blocks.shape[0])
+    ]
+    for copy in copies:
+        copy.start()
+    for copy in copies:
+        copy.wait()
 
 
 def per_device(features, brick_state, neighbor, w_first, b_first, w_second, b_second):
@@ -290,19 +308,19 @@
     matrix = VMEM((3 * channels, 9 * channels), kind)
     column = VMEM((channels, HALF), jnp.float32)
     dma = pltpu.SemaphoreType.DMA
-    return pl.pallas_call(
+    blocks = pl.pallas_call(
         body,
-        out_shape=jax.ShapeDtypeStruct(features.shape, kind),
+        out_shape=VMEM(features.shape, kind),
         in_specs=[scalar, scalar, anywhere, anywhere, whole, anywhere, whole],
-        out_specs=anywhere,
+        out_specs=whole,
         scratch_shapes=[
-            brick_set, brick_set, brick_set,
+            brick_set, brick_set,
             VMEM((bricks, EDGE + 2, 3 * channels, SLAB), kind),
             *[plane_set] * 6,
             VMEM(w_first.shape, kind), VMEM(w_second.shape, kind),
             matrix, matrix, column, column,
-            dma, dma((2,)), dma((bricks,)),
-            dma((4,)), dma((4,)), dma((4, bricks)), dma((4, bricks)),
+            dma((bricks,)), dma((2,)), dma((2,)), dma((2,)),
+            dma((2, bricks)), dma((2, bricks)), dma((4, bricks)), dma((4, bricks)),
         ],
         compiler_params=pltpu.CompilerParams(
             collective_id=0, has_side_effects=True, vmem_limit_bytes=LIMIT
@@ -312,6 +330,15 @@
         brick_state, neighbor, features,
         w_first, b_first.reshape(1, channels), w_second, b_second.reshape(1, channels),
     )
+    return pl.pallas_call(
+        store_body,
+        out_shape=jax.ShapeDtypeStruct(features.shape, kind),
+        in_specs=[whole],
+        out_specs=anywhere,
+        scratch_shapes=[dma((bricks,))],
+        compiler_params=pltpu.CompilerParams(vmem_limit_bytes=16 * 2**20),
+        name="store_blocks",
+    )(blocks)
 
 
 def solution(mesh):

time: 46.9 us -> 43 us (0.917)
  local copies, waits for them, and re-layouts: 3.91 us -> 0 us
    unnamed x1 -> x0, local copies, waits for them, and re-layouts: 3.91 us -> none
    pallas_call x1 -> x2, Pallas kernels: 42.6 us -> 42.8 us  [the longest x1 41 us: per_device(): pl.pallas_call(body, out_shape=VMEM(features.shape, kind), in_specs=[scal...]
where the time goes in v3:
time: 43 us; the launch traced here: 42.8 us
  Pallas kernels  42.8 us (100%)
    pallas_call x1, Pallas kernels, per_device(): pl.pallas_call(body, out_shape=VMEM(features.shape, kind), in_specs=[scal...  41 us
    pallas_call x1, Pallas kernels, per_device(): pl.pallas_call(store_body, out_shape=jax.ShapeDtypeStruct(features.shape,...  1.71 us

profile of v3, /device:TPU:64, one launch (start us, length us, event | category | flops | bytes accessed | tf_op | source)
XLA Modules:
  0.0 42.8 jit_solution(6629633715938573838)
XLA Ops:
  0.0 41.0 %residual_pair.1.blocks = bf16[6,64,4096]{2,1,0:T(8,128)(2,1)S(1)} custom-call(s32[6]{0:T(128)} %state.1, s32[6,6]{1,0:T(8,128)} %neighbor.1, bf16[6,64,4096]{2,1,0:T(8,128)(2,1)} %features.1, bf16[27,64,64]{2,1,0:T(8,128)(2,1)} %w_first.1, f32[1,64]{1,0:T(1,128)} %bitcast.2, bf16[27,64,64]{2,1,0:T(8,128)(2,1)} %w_second.1, f32[1,64]{1,0:T(1,128)} %bitcast.3), custom_call_target="tpu_custom_call" | custom-call | tf_op jit(solution)/shard_map/residual_pair/pallas_call | solution.py:311
  41.1 1.7 %store_blocks.1 = bf16[6,64,4096]{2,1,0:T(8,128)(2,1)} custom-call(bf16[6,64,4096]{2,1,0:T(8,128)(2,1)S(1)} %residual_pair.1.blocks), custom_call_target="tpu_custom_call" | custom-call | tf_op jit(solution)/shard_map/store_blocks/pallas_call | solution.py:333

commit v4 on v3

--- a/solution.py
+++ b/solution.py
@@ -52,14 +52,6 @@
     return down, half, up
 
 
-def put(stacked, b, x, left, right):
-    channels = left[0].shape[0]
-    for dz in range(3):
-        rows = slice(dz * channels, (dz + 1) * channels)
-        stacked[b, x + 1, rows, :HALF] = left[dz]
-        stacked[b, x + 1, rows, HALF:] = right[dz]
-
-
 def stack_brick(values, neighbor, b, stacked):
     bricks, channels = values.shape[0], values.shape[1]
     zero = jnp.zeros((channels, HALF), values.dtype)
@@ -70,23 +62,34 @@
 
     has_below, below = z_neighbor(4)
     has_above, above = z_neighbor(5)
-    for x in range(EDGE):
-        shifts = []
-        for half in range(2):
-            span = slice(x * SLAB + half * HALF, x * SLAB + (half + 1) * HALF)
-            low = turn(values[below, :, span], 1 - EDGE)
-            high = turn(values[above, :, span], EDGE - 1)
-            shifts.append(
-                z_shifted(
-                    values[b, :, span],
-                    jnp.where(has_below, low, zero),
-                    jnp.where(has_above, high, zero),
-                )
-            )
-        put(stacked, b, x, *shifts)
-
-
-def conv_brick(values, halo_x, halo_y, own_y, neighbor, b, stacked, matrix, bias, finish):
+
+    def shifts(x, half):
+        span = slice(x * SLAB + half * HALF, x * SLAB + (half + 1) * HALF)
+        low = turn(values[below, :, span], 1 - EDGE)
+        high = turn(values[above, :, span], EDGE - 1)
+        return z_shifted(
+            values[b, :, span],
+            jnp.where(has_below, low, zero),
+            jnp.where(has_above, high, zero),
+        )
+
+    for half in range(2):
+        columns = slice(half * HALF, (half + 1) * HALF)
+        before, first = None, shifts(0, half)
+        for pair in range(EDGE // 2):
+            second = shifts(2 * pair + 1, half)
+            after = shifts(2 * pair + 2, half) if pair < EDGE // 2 - 1 else None
+            for dz in range(3):
+                rows = slice(dz * channels, (dz + 1) * channels)
+                d1, d2 = first[dz], second[dz]
+                stacked[b, pair, 0, rows, columns] = -d2 if before is None else before[dz] - d2
+                stacked[b, pair, 1, rows, columns] = d1 + d2
+                stacked[b, pair, 2, rows, columns] = d2 - d1
+                stacked[b, pair, 3, rows, columns] = d1 if after is None else d1 - after[dz]
+            before, first = second, after
+
+
+def conv_brick(values, halo_x, halo_y, own_y, neighbor, b, stacked, matrix, factors, bias, finish):
     bricks, channels = values.shape[0], values.shape[1]
     lane = lanes(channels)
     zero = jnp.zeros((channels, HALF), values.dtype)
@@ -116,14 +119,25 @@
         return jnp.dot(rows, tall, preferred_element_type=jnp.float32)
 
     low_y, high_y = y_face(2), y_face(3)
-    for x, index in ((-1, 0), (EDGE, 1)):
+    for index, pair, part in ((0, 0, 0), (1, EDGE // 2 - 1, 3)):
         inner = at_x(EDGE - 1 if index == 0 else 0)
         slab = face(index, lambda k, inner=inner: values[k, :, inner], halo_x)
-        left = z_shifted(slab[:, :HALF], zero, zero)
-        put(stacked, b, x, left, z_shifted(slab[:, HALF:], zero, zero))
+        for half in range(2):
+            columns = slice(half * HALF, (half + 1) * HALF)
+            for dz, shifted in enumerate(z_shifted(slab[:, columns], zero, zero)):
+                rows = slice(dz * channels, (dz + 1) * channels)
+                if index == 0:
+                    stacked[b, pair, part, rows, columns] += shifted
+                else:
+                    stacked[b, pair, part, rows, columns] -= shifted
     for x in range(EDGE):
-        taps = stacked[b, x : x + 3].reshape(9 * channels, SLAB)
-        sums = jnp.dot(matrix[...], taps, preferred_element_type=jnp.float32)
+        if x % 2 == 0:
+            m = [
+                jnp.dot(factors[j], stacked[b, x // 2, j], preferred_element_type=jnp.float32)
+                for j in range(4)
+            ]
+            two = (m[0] + m[1] + m[2], m[1] - m[2] - m[3])
+        sums = two[x % 2]
         before, middle, after = (sums[i * channels : (i + 1) * channels] for i in range(3))
         plane_half = slice(x // 8 * HALF, (x // 8 + 1) * HALF)
         place = (x % 8) * EDGE
@@ -139,7 +153,7 @@
             finish(slice(x * SLAB + half * HALF, x * SLAB + (half + 1) * HALF), total)
 
 
-def prepare(weights, bias, matrix, column_out):
+def prepare(weights, bias, matrix, factors, column_out):
     channels = weights.shape[1]
     for dy in range(3):
         blocks = [weights[9 * (j // 3) + 3 * dy + j % 3] for j in range(9)]
@@ -148,6 +162,13 @@
             columns = slice(pair * 2 * channels, (pair + 1) * 2 * channels)
             matrix[rows, columns] = jnp.concatenate(blocks[2 * pair : 2 * pair + 2], axis=1)
         matrix[rows, 8 * channels : 9 * channels] = blocks[8]
+    for dy in range(3):
+        rows = slice(dy * channels, (dy + 1) * channels)
+        for dz in range(3):
+            g0, g1, g2 = (weights[9 * dx + 3 * dy + dz].astype(jnp.float32) for dx in range(3))
+            columns = slice(dz * channels, (dz + 1) * channels)
+            for j, g in enumerate((g0, 0.5 * (g0 + g1 + g2), 0.5 * (g0 - g1 + g2), g2)):
+                factors[j, rows, columns] = g.astype(weights.dtype)
     row = lax.broadcasted_iota(jnp.int32, (channels, channels), 0)
     column = lax.broadcasted_iota(jnp.int32, (channels, channels), 1)
     wide = jnp.broadcast_to(bias[...], (channels, channels))
@@ -159,7 +180,7 @@
     state, neighbor, features, w_first, b_first, w_second, b_second, out,
     staged, hidden, stacked,
     planes_1, halo_x_1, halo_y_1, planes_2, halo_x_2, halo_y_2,
-    weights_1, weights_2, matrix_1, matrix_2, bias_1, bias_2,
+    weights_1, weights_2, matrix_1, matrix_2, factors_1, factors_2, bias_1, bias_2,
     load_sem, weight_sem, send_x, recv_x, send_sem_1, recv_sem_1, send_sem_2, recv_sem_2,
 ):
     bricks = staged.shape[0]
@@ -226,8 +247,8 @@
 
     for copy in weight_loads:
         copy.wait()
-    prepare(weights_1, b_first, matrix_1, bias_1)
-    prepare(weights_2, b_second, matrix_2, bias_2)
+    prepare(weights_1, b_first, matrix_1, factors_1, bias_1)
+    prepare(weights_2, b_second, matrix_2, factors_2, bias_2)
 
     @pl.loop(0, bricks)
     def _(b):
@@ -258,7 +279,7 @@
             hidden[b, :, span] = jnp.where(live, jnp.maximum(total, 0.0), 0.0).astype(kind)
 
         conv_brick(
-            staged, halo_x_1, halo_y_1, planes_1, neighbor, b, stacked, matrix_1, bias_1, finish
+            staged, halo_x_1, halo_y_1, planes_1, neighbor, b, stacked, matrix_1, factors_1, bias_1, finish
         )
         outer_rows(hidden, b, planes_2)
         for copy in hidden_copies(b):
@@ -283,7 +304,7 @@
             out[b, :, span] = jnp.where(live, jnp.maximum(summed, 0.0), 0.0).astype(kind)
 
         conv_brick(
-            hidden, halo_x_2, halo_y_2, planes_2, neighbor, b, stacked, matrix_2, bias_2, finish
+            hidden, halo_x_2, halo_y_2, planes_2, neighbor, b, stacked, matrix_2, factors_2, bias_2, finish
         )
 
 
@@ -306,6 +327,7 @@
     brick_set = VMEM(features.shape, kind)
     plane_set = VMEM((2, bricks, channels, SLAB), kind)
     matrix = VMEM((3 * channels, 9 * channels), kind)
+    factors = VMEM((4, 3 * channels, 3 * channels), kind)
     column = VMEM((channels, HALF), jnp.float32)
     dma = pltpu.SemaphoreType.DMA
     blocks = pl.pallas_call(
@@ -315,10 +337,10 @@
         out_specs=whole,
         scratch_shapes=[
             brick_set, brick_set,
-            VMEM((bricks, EDGE + 2, 3 * channels, SLAB), kind),
+            VMEM((bricks, EDGE // 2, 4, 3 * channels, SLAB), kind),
             *[plane_set] * 6,
             VMEM(w_first.shape, kind), VMEM(w_second.shape, kind),
-            matrix, matrix, column, column,
+            matrix, matrix, factors, factors, column, column,
             dma((bricks,)), dma((2,)), dma((2,)), dma((2,)),
             dma((2, bricks)), dma((2, bricks)), dma((4, bricks)), dma((4, bricks)),
         ],

time: 43 us -> 40.4 us (0.940)
  Pallas kernels: 42.8 us -> 40.2 us
    pallas_call x1, Pallas kernels: 41 us -> 38.5 us  [per_device(): pl.pallas_call(body, out_shape=VMEM(features.shape, kind), in_specs=[scal...]
where the time goes in v4:
time: 40.4 us; the launch traced here: 40.2 us
  Pallas kernels  40.2 us (100%)
    pallas_call x1, Pallas kernels, per_device(): pl.pallas_call(body, out_shape=VMEM(features.shape, kind), in_specs=[scal...  38.5 us
    pallas_call x1, Pallas kernels, per_device(): pl.pallas_call(store_body, out_shape=jax.ShapeDtypeStruct(features.shape,...  1.71 us

profile of v4, /device:TPU:64, one launch (start us, length us, event | category | flops | bytes accessed | tf_op | source)
XLA Modules:
  0.0 40.2 jit_solution(4183640892656541072)
XLA Ops:
  0.0 38.5 %residual_pair.1.blocks = bf16[6,64,4096]{2,1,0:T(8,128)(2,1)S(1)} custom-call(s32[6]{0:T(128)} %state.1, s32[6,6]{1,0:T(8,128)} %neighbor.1, bf16[6,64,4096]{2,1,0:T(8,128)(2,1)} %features.1, bf16[27,64,64]{2,1,0:T(8,128)(2,1)} %w_first.1, f32[1,64]{1,0:T(1,128)} %bitcast.2, bf16[27,64,64]{2,1,0:T(8,128)(2,1)} %w_second.1, f32[1,64]{1,0:T(1,128)} %bitcast.3), custom_call_target="tpu_custom_call" | custom-call | tf_op jit(solution)/shard_map/residual_pair/pallas_call | solution.py:333
  38.5 1.7 %store_blocks.1 = bf16[6,64,4096]{2,1,0:T(8,128)(2,1)} custom-call(bf16[6,64,4096]{2,1,0:T(8,128)(2,1)S(1)} %residual_pair.1.blocks), custom_call_target="tpu_custom_call" | custom-call | tf_op jit(solution)/shard_map/store_blocks/pallas_call | solution.py:355
